TPU v7x, 512 devices: a whole 4x8x8 slice. The times are simulated.
512 devices in a mesh: dp: 4 (over x), fsdp: 128 (over z, y, core).
Axes of the slice: x: 4, y: 8, z: 8, core: 2. Of those that a mesh axis runs over, the one named last changes fastest.
Arguments:
- grad_parts: bfloat16 [4, 384, 256, 256], P('dp', None, 'fsdp'), may hold values from -4 to 4
- owner_slot: int32 [4, 96], replicated, may hold values from 0 to 255, as said below
- moment: bfloat16 [1024, 256, 256], P(('dp', 'fsdp')), may hold values from -6 to 6
- second: float32 [1024, 256, 256], P(('dp', 'fsdp')), may hold values from 0.2 to 5
- gram_left: float32 [1024, 256, 256], P(('dp', 'fsdp')), may hold values from -24 to 24
- gram_right: float32 [1024, 256, 256], P(('dp', 'fsdp')), may hold values from -24 to 24
- basis_left: bfloat16 [1024, 256, 256], P(('dp', 'fsdp')), may hold values from -0.375 to 0.375
- basis_right: bfloat16 [1024, 256, 256], P(('dp', 'fsdp')), may hold values from -0.375 to 0.375
Outputs:
- new_moment: bfloat16 [1024, 256, 256], P(('dp', 'fsdp'))
- new_second: float32 [1024, 256, 256], P(('dp', 'fsdp'))
- new_left: float32 [1024, 256, 256], P(('dp', 'fsdp'))
- new_right: float32 [1024, 256, 256], P(('dp', 'fsdp'))
- update: bfloat16 [384, 256, 256], P(None, 'fsdp')
Inputs may be any that keep to these rules, and one draw needn't show every extreme that they name: `owner_slot`: in each row the 96 entries are distinct; entry o * 2 + c names slot c of owner o along fsdp; in every row some owner receives 2 blocks.
All inputs are finite; a program needn't handle non-finite values.
Results may differ from a plain program's by a relative error of at most 0.01.
Values may be sent and summed in bfloat16 or wider, within the bound.
A program may use at most 64 MiB of HBM per device.

v0:
```python
import jax
import jax.numpy as jnp
from jax import lax
from jax.sharding import PartitionSpec as P


def rotate_slots(slot_grads, moment, second, gram_left, gram_right, basis_left, basis_right):
    rounded = slot_grads.astype(jnp.bfloat16)
    halfway = jnp.einsum(
        "kij,kil->kjl", basis_left, rounded, preferred_element_type=jnp.float32
    ).astype(jnp.bfloat16)
    rotated = jnp.einsum("kjl,klm->kjm", halfway, basis_right, preferred_element_type=jnp.float32)
    new_left = 0.95 * gram_left + 0.05 * jnp.einsum(
        "kij,klj->kil", slot_grads, slot_grads, precision=lax.Precision.HIGHEST
    )
    new_right = 0.95 * gram_right + 0.05 * jnp.einsum(
        "kji,kjl->kil", slot_grads, slot_grads, precision=lax.Precision.HIGHEST
    )
    first_moment = 0.95 * moment.astype(jnp.float32) + 0.05 * rotated
    new_second = 0.95 * second + 0.05 * rotated * rotated
    direct = (first_moment / (jnp.sqrt(new_second) + 1e-08)).astype(jnp.bfloat16)
    returned = jnp.einsum(
        "kij,kjl->kil", basis_left, direct, preferred_element_type=jnp.float32
    ).astype(jnp.bfloat16)
    slot_update = jnp.einsum(
        "kil,kml->kim", returned, basis_right, preferred_element_type=jnp.float32
    ).astype(jnp.bfloat16)
    return (first_moment.astype(jnp.bfloat16), new_second, new_left, new_right, slot_update)


def on_device(
    grad_parts, owner_slot, moment, second, gram_left, gram_right, basis_left, basis_right
):
    dp_count = lax.axis_size("dp")
    fsdp_count = lax.axis_size("fsdp")
    capacity = moment.shape[0]
    block_side = moment.shape[2]
    row_count = grad_parts.shape[2]
    replica = lax.axis_index("dp")
    targets = lax.dynamic_index_in_dim(owner_slot, replica, 0, keepdims=False)
    owner_rank = owner_slot // capacity
    within = owner_slot % capacity
    routed_index = (
        owner_rank * (dp_count * capacity)
        + jnp.arange(dp_count, dtype=jnp.int32)[:, None] * capacity
        + within
    ).reshape(-1)
    summed = lax.psum_scatter(
        grad_parts[0].astype(jnp.float32).astype(jnp.bfloat16),
        "dp",
        scatter_dimension=0,
        tiled=True,
    ).astype(jnp.float32)
    outgoing = (
        jnp.zeros((fsdp_count * capacity, row_count, block_side), jnp.float32)
        .at[targets]
        .set(summed)
    )
    outgoing = outgoing.reshape(fsdp_count, capacity, row_count, block_side)
    arrived = lax.all_to_all(
        outgoing.astype(jnp.bfloat16), "fsdp", split_axis=0, concat_axis=2, tiled=True
    ).astype(outgoing.dtype)
    slot_grads = arrived.reshape(capacity, block_side, block_side)
    new_moment, new_second, new_left, new_right, slot_update = rotate_slots(
        slot_grads, moment, second, gram_left, gram_right, basis_left, basis_right
    )
    everyone = lax.all_gather(slot_update, "dp", axis=0, tiled=True)
    pieces = everyone.reshape(dp_count * capacity, fsdp_count, row_count, block_side)
    returned = lax.all_to_all(pieces, "fsdp", split_axis=1, concat_axis=0, tiled=True)
    update = returned[:, 0][routed_index]
    return (new_moment, new_second, new_left, new_right, update)


def solution(mesh):
    return jax.shard_map(
        on_device,
        mesh=mesh,
        in_specs=(
            P("dp", None, "fsdp", None),
            P(),
            P(("dp", "fsdp"), None, None),
            P(("dp", "fsdp"), None, None),
            P(("dp", "fsdp"), None, None),
            P(("dp", "fsdp"), None, None),
            P(("dp", "fsdp"), None, None),
            P(("dp", "fsdp"), None, None),
        ),
        out_specs=(
            P(("dp", "fsdp"), None, None),
            P(("dp", "fsdp"), None, None),
            P(("dp", "fsdp"), None, None),
            P(("dp", "fsdp"), None, None),
            P(None, "fsdp", None),
        ),
        check_vma=False,
    )
```

profile of v0, /device:TPU:1, one launch (start us, length us, event | category | flops | bytes accessed | tf_op | source)
XLA Modules:
  0.0 186.8 jit_solution(5582185844776499052)
XLA Ops:
  7.2 0.0 copy-start
  7.2 0.0 all-reduce.3.cloned.1.call-start
  7.2 0.7 all-reduce.3.cloned.1.call-update
  7.9 0.0 all-gather.2.cloned.1.call-start
  8.0 1.3 dynamic-slice
  9.2 0.0 copy-start.7
  9.9 0.0 copy-done.7
  9.9 56.7 %all-reduce.3.cloned.1.call-done = bf16[384,2,256]{2,1,0:T(2,128)(2,1)} async-done(((bf16[384,2,256]{2,1,0:T(2,128)(2,1)}), bf16[384,2,256]{2,1,0:T(2,128)(2,1)}) %all-reduce.3.cloned.1.call-update) | async-done | bytes 393232
  66.6 1.0 dynamic-slice_convert_fusion
  67.6 0.1 broadcast_in_dim.2
  67.8 3.4 %scatter_fusion = f32[256,2,256]{2,1,0:T(2,128)S(1)} fusion(f32[256,2,256]{2,1,0:T(2,128)S(1)} %broadcast_in_dim.2, s32[96]{0:T(128)S(1)} %fusion.19, f32[96,2,256]{2,1,0:T(2,128)S(1)} %dynamic-slice_convert_fusion), kind=kCustom, calls=%fused_computation.1 | custom fusion | bytes 590208 | tf_op jit(solution)/shard_map/scatter | solution.py:57
  71.1 0.2 convert_element_type.38
  71.3 31.5 %all_to_all.33 = bf16[128,2,2,256]{3,2,1,0:T(2,128)(2,1)S(1)} all-to-all(bf16[128,2,2,256]{3,2,1,0:T(2,128)(2,1)S(1)} %bitcast.29), channel_id=1, replica_groups=mesh['dp'=4,'fsdp'=128] {'fsdp'}, dimensions={0} | all-to-all | bytes 524288 | tf_op jit(solution)/shard_map/all_to_all | solution.py:60
  102.8 0.0 copy-start.3
  102.8 0.2 copy.28
  103.0 0.0 copy-start.5
  103.0 0.0 copy-start.6
  103.1 0.2 copy.29
  103.2 0.0 copy-done
  103.2 0.6 copy-done.3
  103.9 0.2 copy-done.5
  104.0 0.1 copy-done.6
  104.1 1.2 fusion.3
  105.3 0.0 copy-start.4
  105.3 1.4 convolution_convert_fusion
  106.7 0.0 copy-done.4
  106.7 0.0 all-gather.2.cloned.1.call-update
  106.7 20.0 %all-gather.2.cloned.1.call-done = bf16[8,256,256]{2,1,0:T(8,128)(2,1)} async-done(((bf16[2,256,256]{2,1,0:T(8,128)(2,1)}), bf16[8,256,256]{2,1,0:T(8,128)(2,1)}) %all-gather.2.cloned.1.call-update) | async-done | bytes 1048592 | tf_op jit(solution)/shard_map/all_gather | solution.py:67
  126.7 2.8 %copy.43 = bf16[8,256,256]{2,0,1:T(8,128)(2,1)} copy(bf16[8,256,256]{2,1,0:T(8,128)(2,1)} %all-gather.2.cloned.1.call-done) | data formatting | bytes 2097152 | tf_op jit(solution)/shard_map/reshape | solution.py:68
  129.6 0.0 copy-start.2
  129.6 15.3 %all-to-all-start.1 = ((bf16[8,128,2,256]{3,0,2,1:T(8,128)(2,1)}), bf16[8,128,2,256]{3,0,2,1:T(8,128)(2,1)S(1)}, u32[]{:S(2)}, u32[]{:S(2)}) async-start(bf16[8,128,2,256]{3,0,2,1:T(8,128)(2,1)} %bitcast.7), calls=%async_computation.1 | async-start | bytes 2097152 | tf_op jit(solution)/shard_map/all_to_all | solution.py:69
  144.9 0.1 fusion.15
  145.0 0.1 reshape.87
  145.1 0.0 copy-done.2
  145.1 0.0 copy-start.1
  145.1 1.1 fusion.1
  146.2 0.0 copy-done.1
  146.2 1.0 fusion
  147.2 28.6 %all-to-all-done.1 = bf16[8,128,2,256]{3,0,2,1:T(8,128)(2,1)S(1)} async-done(((bf16[8,128,2,256]{3,0,2,1:T(8,128)(2,1)}), bf16[8,128,2,256]{3,0,2,1:T(8,128)(2,1)S(1)}, u32[]{:S(2)}, u32[]{:S(2)}) %all-to-all-start.1) | async-done | bytes 1048608 | tf_op jit(solution)/shard_map/all_to_all | solution.py:69
  175.8 0.1 copy.49
  175.9 1.1 copy.39
  177.0 3.0 %gather_fusion = bf16[384,2,256]{2,1,0:T(2,128)(2,1)} fusion(bf16[1024,2,256]{2,1,0:T(2,128)(2,1)S(1)} %copy.39, s32[1024]{0:T(1024)S(1)} %pad_clamp_fusion), kind=kCustom, calls=%fused_computation | custom fusion | bytes 787968 | tf_op jit(solution)/shard_map/gather | solution.py:70
  (4 shorter events, 0.0 us)
Async XLA Ops:
  7.2 96.1 %copy-start = (bf16[2,256,256]{2,1,0:T(8,128)(2,1)S(1)}, bf16[2,256,256]{2,1,0:T(8,128)(2,1)}, u32[]{:S(2)}) copy-start(bf16[2,256,256]{2,1,0:T(8,128)(2,1)} %param.15) | copy-start | bytes 786436
  7.2 59.5 %all-reduce.3.cloned.1.call-start = ((), (), s32[]{:S(2)}) async-start(), calls=%async_computation.3 | async-start | bytes 786432
  7.9 118.8 %all-gather.2.cloned.1.call-start = ((), (), s32[]{:S(2)}) async-start(), calls=%async_computation.2 | async-start | bytes 1310720 | tf_op jit(solution)/shard_map/all_gather | solution.py:67
  9.2 0.7 copy-start.7
  102.8 1.0 copy-start.3
  103.0 1.0 copy-start.5
  103.0 1.1 copy-start.6
  105.3 1.4 copy-start.4
  129.6 15.5 %copy-start.2 = (f32[2,256,256]{2,1,0:T(8,128)S(1)}, f32[2,256,256]{2,1,0:T(8,128)}, u32[]{:S(2)}) copy-start(f32[2,256,256]{2,1,0:T(8,128)} %param.12) | copy-start | bytes 1572868
  129.6 46.2 %all-to-all-start.1 = ((bf16[8,128,2,256]{3,0,2,1:T(8,128)(2,1)}), bf16[8,128,2,256]{3,0,2,1:T(8,128)(2,1)S(1)}, u32[]{:S(2)}, u32[]{:S(2)}) async-start(bf16[8,128,2,256]{3,0,2,1:T(8,128)(2,1)} %bitcast.7), calls=%async_computation.1 | async-start | bytes 2097152 | tf_op jit(solution)/shard_map/all_to_all | solution.py:69
  145.1 1.1 copy-start.1
Sparse Core Ops, SparseCore 0:
  10.4 56.2 all-reduce.2
  106.9 19.8 all-gather.1
where the time goes:
time: 187 us
  waiting for transfers between devices  106 us (57%)
  blocking collectives  31.5 us (17%)
  starting transfers between devices  15.4 us (8%)
  between operations  14.8 us (8%)
  local copies, waits for them, and re-layouts  13.1 us (7%)
  matrix products  4.71 us (3%)
    unnamed x3, waiting for transfers between devices  57.4 us
    all_to_all x1, blocking collectives, on_device(): lax.all_to_all(outgoing.astype(jnp.bfloat16), 'fsdp', split_axis=0, conca...  31.5 us
    all_to_all x1, waiting for transfers between devices, on_device(): lax.all_to_all(pieces, 'fsdp', split_axis=1, concat_axis=0, tiled=True)  28.6 us
    all_gather x1, waiting for transfers between devices, on_device(): everyone = lax.all_gather(slot_update, 'dp', axis=0, tiled=True)  20 us
    all_to_all x1, starting transfers between devices, on_device(): lax.all_to_all(pieces, 'fsdp', split_axis=1, concat_axis=0, tiled=True)  15.3 us
  transfers between devices with their start and end apart: 3, of which 3 were waited for; matrix products, arithmetic and copies ran while one was open for 2% of the time, Pallas kernels for 0%

commit v1 on v0

v1 whole, which is shorter than its diff:
```python
import functools

import jax
import jax.numpy as jnp
from jax import lax
from jax.experimental import pallas as pl
from jax.experimental.pallas import tpu as pltpu
from jax.sharding import PartitionSpec as P

MESH = pl.DeviceIdType.MESH
UNROLL = 8
TILE = 8


def contract(a, b, a_dim, b_dim):
    return lax.dot_general(
        a, b, (((a_dim,), (b_dim,)), ((), ())), preferred_element_type=jnp.float32
    )


def soap_kernel(
    dp_count,
    fsdp_count,
    block_of,
    owner_slot,
    grad_parts,
    moment,
    second,
    gram_left,
    gram_right,
    basis_left,
    basis_right,
    new_moment,
    new_second,
    new_left,
    new_right,
    update,
    moment_v,
    second_v,
    left_v,
    right_v,
    basis_left_v,
    basis_right_v,
    partials,
    summed,
    outgoing,
    incoming,
    slot_grad,
    slot_update,
    returning,
    returned,
    picked,
    load_sems,
    store_sems,
    partial_send,
    partial_recv,
    out_send,
    in_recv,
    back_send,
    back_recv,
    gather_send,
    gather_recv,
):
    dp = lax.axis_index("dp")
    me = lax.axis_index("fsdp")
    capacity, side = moment.shape[0], moment.shape[1]
    group_blocks = owner_slot.shape[1]
    rows = grad_parts.shape[2]

    own_partial = pltpu.make_async_copy(
        grad_parts.at[0, pl.ds(dp * group_blocks, group_blocks)], partials.at[0], load_sems.at[6]
    )
    own_partial.start()
    loads = [
        pltpu.make_async_copy(src, dst, load_sems.at[i])
        for i, (src, dst) in enumerate(
            (
                (basis_left, basis_left_v),
                (basis_right, basis_right_v),
                (moment, moment_v),
                (second, second_v),
                (gram_left, left_v),
                (gram_right, right_v),
            )
        )
    ]
    for load in loads:
        load.start()

    barrier = pltpu.get_barrier_semaphore()
    for k in range(1, dp_count):
        pl.semaphore_signal(
            barrier, inc=1, device_id=(lax.rem(dp + k, dp_count), me), device_id_type=MESH
        )

    def greet(k, carry):
        pl.semaphore_signal(
            barrier, inc=1, device_id=(dp, lax.rem(me + k, fsdp_count)), device_id_type=MESH
        )
        return carry

    lax.fori_loop(1, fsdp_count, greet, 0)
    pl.semaphore_wait(barrier, dp_count - 1 + fsdp_count - 1)

    partial_copies = []
    for k in range(1, dp_count):
        target = lax.rem(dp + k, dp_count)
        copy = pltpu.make_async_remote_copy(
            src_ref=grad_parts.at[0, pl.ds(target * group_blocks, group_blocks)],
            dst_ref=partials.at[k],
            send_sem=partial_send.at[k - 1],
            recv_sem=partial_recv.at[k - 1],
            device_id=(target, me),
            device_id_type=MESH,
        )
        copy.start()
        partial_copies.append(copy)
    summed[group_blocks] = jnp.zeros(summed.shape[1:], summed.dtype)
    own_partial.wait()
    for copy in partial_copies:
        copy.wait_recv()

    def add_up(i, carry):
        here = pl.ds(i * UNROLL, UNROLL)
        total = partials[0, here].astype(jnp.float32)
        for k in range(1, dp_count):
            total = total + partials[k, here].astype(jnp.float32)
        summed[here] = total.astype(jnp.bfloat16)
        return carry

    lax.fori_loop(0, group_blocks // UNROLL, add_up, 0)

    def send_out(k, carry):
        owner = lax.rem(me + k, fsdp_count)
        for c in range(capacity):
            slot = owner * capacity + c
            outgoing[slot] = summed[block_of[dp, slot]]
        here = pl.ds(owner * capacity, capacity)
        pltpu.make_async_remote_copy(
            src_ref=outgoing.at[here],
            dst_ref=incoming.at[pl.ds(me * capacity, capacity)],
            send_sem=out_send,
            recv_sem=in_recv,
            device_id=(dp, owner),
            device_id_type=MESH,
        ).start()
        return carry

    lax.fori_loop(1, fsdp_count, send_out, 0)
    for c in range(capacity):
        slot = me * capacity + c
        incoming[slot] = summed[block_of[dp, slot]]

    others = pl.ds(0, (fsdp_count - 1) * capacity)
    out_all = pltpu.make_async_remote_copy(
        src_ref=outgoing.at[others],
        dst_ref=incoming.at[others],
        send_sem=out_send,
        recv_sem=in_recv,
        device_id=(dp, lax.rem(me + 1, fsdp_count)),
        device_id_type=MESH,
    )
    out_all.wait_recv()

    per_tile = slot_grad.shape[2] // rows

    def unpack(i, carry):
        for u in range(per_tile):
            for c in range(capacity):
                slot_grad[c, i, u * rows : (u + 1) * rows, :] = incoming[
                    (i * per_tile + u) * capacity + c
                ].astype(jnp.float32)
        return carry

    lax.fori_loop(0, slot_grad.shape[1], unpack, 0)

    for load in loads:
        load.wait()

    rounded = [
        slot_grad[c].reshape(side, side).astype(jnp.bfloat16) for c in range(capacity)
    ]
    for c in range(capacity):
        halfway = contract(basis_left_v[c], rounded[c], 0, 0).astype(jnp.bfloat16)
        rotated = contract(halfway, basis_right_v[c], 1, 0)
        first_moment = 0.95 * moment_v[c].astype(jnp.float32) + 0.05 * rotated
        moment_v[c] = first_moment.astype(jnp.bfloat16)
        second_moment = 0.95 * second_v[c] + 0.05 * rotated * rotated
        second_v[c] = second_moment
        direct = (first_moment / (jnp.sqrt(second_moment) + 1e-8)).astype(jnp.bfloat16)
        back = contract(basis_left_v[c], direct, 1, 0).astype(jnp.bfloat16)
        slot_update[c] = contract(back, basis_right_v[c], 1, 1).reshape(slot_update.shape[1:])

    def pack(i, carry):
        for u in range(per_tile):
            for c in range(capacity):
                returning[(i * per_tile + u) * capacity + c] = slot_update[
                    c, i, u * rows : (u + 1) * rows, :
                ].astype(jnp.bfloat16)
        return carry

    lax.fori_loop(0, slot_update.shape[1], pack, 0)

    def send_back(k, carry):
        target = lax.rem(me + k, fsdp_count)
        here = pl.ds(target * capacity, capacity)
        pltpu.make_async_remote_copy(
            src_ref=returning.at[here],
            dst_ref=returned.at[pl.ds(me * capacity, capacity)],
            send_sem=back_send,
            recv_sem=back_recv,
            device_id=(dp, target),
            device_id_type=MESH,
        ).start()
        return carry

    lax.fori_loop(1, fsdp_count, send_back, 0)
    for c in range(capacity):
        returned[me * capacity + c] = returning[me * capacity + c]

    stores = [
        pltpu.make_async_copy(moment_v, new_moment, store_sems.at[0]),
        pltpu.make_async_copy(second_v, new_second, store_sems.at[1]),
        pltpu.make_async_copy(left_v, new_left, store_sems.at[2]),
        pltpu.make_async_copy(right_v, new_right, store_sems.at[3]),
    ]
    stores[0].start()
    stores[1].start()
    for c in range(capacity):
        left_v[c] = 0.95 * left_v[c] + 0.05 * contract(rounded[c], rounded[c], 1, 1)
        right_v[c] = 0.95 * right_v[c] + 0.05 * contract(rounded[c], rounded[c], 0, 0)
    stores[2].start()
    stores[3].start()

    back_all = pltpu.make_async_remote_copy(
        src_ref=returning.at[others],
        dst_ref=returned.at[others],
        send_sem=back_send,
        recv_sem=back_recv,
        device_id=(dp, lax.rem(me + 1, fsdp_count)),
        device_id_type=MESH,
    )
    back_all.wait_recv()

    def pick(i, carry):
        for u in range(UNROLL):
            j = i * UNROLL + u
            picked[j] = returned[owner_slot[dp, j]]
        return carry

    lax.fori_loop(0, group_blocks // UNROLL, pick, 0)

    mine = pl.ds(dp * group_blocks, group_blocks)
    gathers = []
    for k in range(1, dp_count):
        copy = pltpu.make_async_remote_copy(
            src_ref=picked,
            dst_ref=update.at[mine],
            send_sem=gather_send.at[k - 1],
            recv_sem=gather_recv.at[k - 1],
            device_id=(lax.rem(dp + k, dp_count), me),
            device_id_type=MESH,
        )
        copy.start()
        gathers.append(copy)
    keep = pltpu.make_async_copy(picked, update.at[mine], store_sems.at[4])
    keep.start()
    out_all.wait_send()
    back_all.wait_send()
    for copy in partial_copies:
        copy.wait_send()
    for store in stores:
        store.wait()
    keep.wait()
    for copy in gathers:
        copy.wait()


def on_device(
    dp_count,
    fsdp_count,
    grad_parts,
    owner_slot,
    moment,
    second,
    gram_left,
    gram_right,
    basis_left,
    basis_right,
):
    capacity, side = moment.shape[0], moment.shape[1]
    blocks, rows = grad_parts.shape[1], grad_parts.shape[2]
    group_blocks = owner_slot.shape[1]
    slots = fsdp_count * capacity
    filled = owner_slot[:, None, :] == jnp.arange(slots, dtype=jnp.int32)[None, :, None]
    block_of = jnp.min(
        jnp.where(filled, jnp.arange(group_blocks, dtype=jnp.int32)[None, None, :], group_blocks),
        axis=2,
    )
    any_spec = pl.BlockSpec(memory_space=pl.ANY)
    smem_spec = pl.BlockSpec(memory_space=pltpu.SMEM)
    square = (capacity, side, side)
    tiled = (capacity, side // TILE, TILE, side)
    dma = pltpu.SemaphoreType.DMA
    return pl.pallas_call(
        functools.partial(soap_kernel, dp_count, fsdp_count),
        out_shape=(
            jax.ShapeDtypeStruct(square, jnp.bfloat16),
            jax.ShapeDtypeStruct(square, jnp.float32),
            jax.ShapeDtypeStruct(square, jnp.float32),
            jax.ShapeDtypeStruct(square, jnp.float32),
            jax.ShapeDtypeStruct((blocks, rows, side), jnp.bfloat16),
        ),
        in_specs=[smem_spec, smem_spec] + [any_spec] * 7,
        out_specs=[any_spec] * 5,
        scratch_shapes=[
            pltpu.VMEM(square, jnp.bfloat16),
            pltpu.VMEM(square, jnp.float32),
            pltpu.VMEM(square, jnp.float32),
            pltpu.VMEM(square, jnp.float32),
            pltpu.VMEM(square, jnp.bfloat16),
            pltpu.VMEM(square, jnp.bfloat16),
            pltpu.VMEM((dp_count, group_blocks, rows, side), jnp.bfloat16),
            pltpu.VMEM((group_blocks + 1, rows, side), jnp.bfloat16),
            pltpu.VMEM((slots, rows, side), jnp.bfloat16),
            pltpu.VMEM((slots, rows, side), jnp.bfloat16),
            pltpu.VMEM(tiled, jnp.float32),
            pltpu.VMEM(tiled, jnp.float32),
            pltpu.VMEM((slots, rows, side), jnp.bfloat16),
            pltpu.VMEM((slots, rows, side), jnp.bfloat16),
            pltpu.VMEM((group_blocks, rows, side), jnp.bfloat16),
            dma((7,)),
            dma((5,)),
            dma((dp_count - 1,)),
            dma((dp_count - 1,)),
            dma,
            dma,
            dma,
            dma,
            dma((dp_count - 1,)),
            dma((dp_count - 1,)),
        ],
        compiler_params=pltpu.CompilerParams(
            collective_id=0, has_side_effects=True, vmem_limit_bytes=32 * 1024 * 1024
        ),
    )(
        block_of,
        owner_slot,
        grad_parts,
        moment,
        second,
        gram_left,
        gram_right,
        basis_left,
        basis_right,
    )


def solution(mesh):
    by_slot = P(("dp", "fsdp"), None, None)
    return jax.shard_map(
        functools.partial(on_device, mesh.shape["dp"], mesh.shape["fsdp"]),
        mesh=mesh,
        in_specs=(P("dp", None, "fsdp", None), P()) + (by_slot,) * 6,
        out_specs=(by_slot,) * 4 + (P(None, "fsdp", None),),
        check_vma=False,
    )
```

time: 187 us -> 67.8 us (0.36)
  waiting for transfers between devices: 106 us -> 0 us
  Pallas kernels: 0 us -> 55.1 us
  blocking collectives: 31.5 us -> 0 us
  starting transfers between devices: 15.4 us -> 0 us
  between operations: 14.8 us -> 0.68 us
  matrix products: 4.71 us -> 0 us
  local copies, waits for them, and re-layouts: 13.1 us -> 10.8 us
    unnamed x3 -> x0, waiting for transfers between devices: 57.4 us -> none
    pallas_call x0 -> x1, Pallas kernels: none -> 55.1 us  [on_device(): pl.pallas_call(functools.partial(soap_kernel, dp_count, fsdp_count), out_...]
    all_to_all x1 -> x0, blocking collectives: 31.5 us -> none  [on_device(): lax.all_to_all(outgoing.astype(jnp.bfloat16), 'fsdp', split_axis=0, conca...]
    all_to_all x1 -> x0, waiting for transfers between devices: 28.6 us -> none  [on_device(): lax.all_to_all(pieces, 'fsdp', split_axis=1, concat_axis=0, tiled=True)]
    all_gather x1 -> x0, waiting for transfers between devices: 20 us -> none  [on_device(): everyone = lax.all_gather(slot_update, 'dp', axis=0, tiled=True)]
    all_to_all x1 -> x0, starting transfers between devices: 15.3 us -> none  [on_device(): lax.all_to_all(pieces, 'fsdp', split_axis=1, concat_axis=0, tiled=True)]
    unnamed x17 -> x21, local copies, waits for them, and re-layouts: 2.17 us -> 10.8 us
    dot_general x4 -> x0, matrix products: 4.71 us -> none  [the longest x1 1.4 us: rotate_slots(): jnp.einsum('kil,kml->kim', returned, basis_right, preferred_element_type=...]
  transfers between devices with their start and end apart: 3 -> 0, of which waited for: 3 -> 0; matrix products, arithmetic and copies ran while one was open for 2% -> 0% of each run, Pallas kernels for 0% -> 0%
where the time goes in v1:
time: 67.8 us; the launch traced here: 67.4 us
  Pallas kernels  55.1 us (81%)
  local copies, waits for them, and re-layouts  10.8 us (16%)
  other arithmetic  0.88 us (1%)
  between operations  0.68 us (1%)
    pallas_call x1, Pallas kernels, on_device(): pl.pallas_call(functools.partial(soap_kernel, dp_count, fsdp_count), out_...  55.1 us
    unnamed x21, local copies, waits for them, and re-layouts  10.8 us

profile of v1, /device:TPU:1, one launch (start us, length us, event | category | flops | bytes accessed | tf_op | source)
XLA Modules:
  0.0 67.4 jit_solution(12010337434235347485)
XLA Ops:
  0.6 0.0 copy-start.7
  0.6 0.9 %select_reduce_fusion.block_of = s32[4,256]{1,0:T(4,128)S(1)} fusion(s32[4,96]{1,0:T(4,128)} %owner_slot.1), kind=kLoop, calls=%fused_computation | loop fusion | flops 293888 | bytes 5632 | tf_op jit(solution)/shard_map/reduce_min | solution.py:296
  1.5 0.0 copy-done.7
  1.5 0.0 copy-start
  1.5 1.0 %copy-done = f32[2,256,256]{2,1,0:T(8,128)S(1)} copy-done((f32[2,256,256]{2,1,0:T(8,128)S(1)}, f32[2,256,256]{2,1,0:T(8,128)}, u32[]{:S(2)}) %copy-start) | copy-done | bytes 524312
  2.6 0.0 copy-start.1
  2.6 1.0 %copy-done.1 = f32[2,256,256]{2,1,0:T(8,128)S(1)} copy-done((f32[2,256,256]{2,1,0:T(8,128)S(1)}, f32[2,256,256]{2,1,0:T(8,128)}, u32[]{:S(2)}) %copy-start.1) | copy-done | bytes 524312
  3.6 0.0 copy-start.2
  3.6 1.0 %copy-done.2 = f32[2,256,256]{2,1,0:T(8,128)S(1)} copy-done((f32[2,256,256]{2,1,0:T(8,128)S(1)}, f32[2,256,256]{2,1,0:T(8,128)}, u32[]{:S(2)}) %copy-start.2) | copy-done | bytes 524312
  4.7 0.0 copy-start.3
  4.7 1.0 %copy-done.3 = bf16[1,384,2,256]{3,2,1,0:T(2,128)(2,1)S(1)} copy-done((bf16[1,384,2,256]{3,2,1,0:T(2,128)(2,1)S(1)}, bf16[1,384,2,256]{3,2,1,0:T(2,128)(2,1)}, u32[]{:S(2)}) %copy-start.3) | copy-done | bytes 393240
  5.7 0.0 copy-start.4
  5.7 0.9 %copy-done.4 = bf16[2,256,256]{2,1,0:T(8,128)(2,1)S(1)} copy-done((bf16[2,256,256]{2,1,0:T(8,128)(2,1)S(1)}, bf16[2,256,256]{2,1,0:T(8,128)(2,1)}, u32[]{:S(2)}) %copy-start.4) | copy-done | bytes 262168
  6.6 0.0 copy-start.5
  6.6 0.9 %copy-done.5 = bf16[2,256,256]{2,1,0:T(8,128)(2,1)S(1)} copy-done((bf16[2,256,256]{2,1,0:T(8,128)(2,1)S(1)}, bf16[2,256,256]{2,1,0:T(8,128)(2,1)}, u32[]{:S(2)}) %copy-start.5) | copy-done | bytes 262168
  7.6 0.0 copy-start.6
  7.6 0.9 %copy-done.6 = bf16[2,256,256]{2,1,0:T(8,128)(2,1)S(1)} copy-done((bf16[2,256,256]{2,1,0:T(8,128)(2,1)S(1)}, bf16[2,256,256]{2,1,0:T(8,128)(2,1)}, u32[]{:S(2)}) %copy-start.6) | copy-done | bytes 262168
  8.5 55.1 %shard_map.119 = (bf16[2,256,256]{2,1,0:T(8,128)(2,1)S(1)}, f32[2,256,256]{2,1,0:T(8,128)S(1)}, f32[2,256,256]{2,1,0:T(8,128)S(1)}, f32[2,256,256]{2,1,0:T(8,128)S(1)}, bf16[384,2,256]{2,1,0:T(2,128)(2,1)S(1)}) custom-call(s32[4,256]{1,0:T(4,128)S(1)} %select_reduce_fusion.block_of, s32[4,96]{1,0:T(4,128)S(1)} %copy-done.7, ...), custom_call_target="tpu_custom_call" | custom-call | tf_op jit(solution)/shard_map/pallas_call | solution.py:305
  63.6 0.7 %copy.18 = bf16[2,256,256]{2,1,0:T(8,128)(2,1)} copy(bf16[2,256,256]{2,1,0:T(8,128)(2,1)S(1)} %get-tuple-element.10) | data formatting | bytes 524288
  64.3 0.8 %copy.19 = f32[2,256,256]{2,1,0:T(8,128)} copy(f32[2,256,256]{2,1,0:T(8,128)S(1)} %get-tuple-element.11) | data formatting | bytes 1048576
  65.1 0.8 %copy.20 = f32[2,256,256]{2,1,0:T(8,128)} copy(f32[2,256,256]{2,1,0:T(8,128)S(1)} %get-tuple-element.12) | data formatting | bytes 1048576
  65.9 0.8 %copy.21 = f32[2,256,256]{2,1,0:T(8,128)} copy(f32[2,256,256]{2,1,0:T(8,128)S(1)} %get-tuple-element.13) | data formatting | bytes 1048576
  66.7 0.7 %copy.22 = bf16[384,2,256]{2,1,0:T(2,128)(2,1)} copy(bf16[384,2,256]{2,1,0:T(2,128)(2,1)S(1)} %get-tuple-element.14) | data formatting | bytes 786432
Async XLA Ops:
  0.6 0.9 %copy-start.7 = (s32[4,96]{1,0:T(4,128)S(1)}, s32[4,96]{1,0:T(4,128)}, u32[]{:S(2)}) copy-start(s32[4,96]{1,0:T(4,128)} %owner_slot.1) | copy-start | bytes 4612
  1.5 1.0 %copy-start = (f32[2,256,256]{2,1,0:T(8,128)S(1)}, f32[2,256,256]{2,1,0:T(8,128)}, u32[]{:S(2)}) copy-start(f32[2,256,256]{2,1,0:T(8,128)} %second.1) | copy-start | bytes 1572868
  2.6 1.0 %copy-start.1 = (f32[2,256,256]{2,1,0:T(8,128)S(1)}, f32[2,256,256]{2,1,0:T(8,128)}, u32[]{:S(2)}) copy-start(f32[2,256,256]{2,1,0:T(8,128)} %gram_left.1) | copy-start | bytes 1572868
  3.6 1.0 %copy-start.2 = (f32[2,256,256]{2,1,0:T(8,128)S(1)}, f32[2,256,256]{2,1,0:T(8,128)}, u32[]{:S(2)}) copy-start(f32[2,256,256]{2,1,0:T(8,128)} %gram_right.1) | copy-start | bytes 1572868
  4.7 1.0 %copy-start.3 = (bf16[1,384,2,256]{3,2,1,0:T(2,128)(2,1)S(1)}, bf16[1,384,2,256]{3,2,1,0:T(2,128)(2,1)}, u32[]{:S(2)}) copy-start(bf16[1,384,2,256]{3,2,1,0:T(2,128)(2,1)} %grad_parts.1) | copy-start | bytes 1179652
  5.7 0.9 %copy-start.4 = (bf16[2,256,256]{2,1,0:T(8,128)(2,1)S(1)}, bf16[2,256,256]{2,1,0:T(8,128)(2,1)}, u32[]{:S(2)}) copy-start(bf16[2,256,256]{2,1,0:T(8,128)(2,1)} %moment.1) | copy-start | bytes 786436
  6.6 0.9 %copy-start.5 = (bf16[2,256,256]{2,1,0:T(8,128)(2,1)S(1)}, bf16[2,256,256]{2,1,0:T(8,128)(2,1)}, u32[]{:S(2)}) copy-start(bf16[2,256,256]{2,1,0:T(8,128)(2,1)} %basis_left.1) | copy-start | bytes 786436
  7.6 0.9 %copy-start.6 = (bf16[2,256,256]{2,1,0:T(8,128)(2,1)S(1)}, bf16[2,256,256]{2,1,0:T(8,128)(2,1)}, u32[]{:S(2)}) copy-start(bf16[2,256,256]{2,1,0:T(8,128)(2,1)} %basis_right.1) | copy-start | bytes 786436

commit v2 on v1

v2 whole, which is shorter than its diff:
```python
import functools
import math

import jax
import jax.numpy as jnp
from jax import lax
from jax.experimental import pallas as pl
from jax.experimental.pallas import tpu as pltpu
from jax.sharding import PartitionSpec as P

MESH = pl.DeviceIdType.MESH
UNROLL = 8
TILE = 8
LANES = 128
LIMIT = 60


def contract(a, b, a_dim, b_dim):
    return lax.dot_general(
        a, b, (((a_dim,), (b_dim,)), ((), ())), preferred_element_type=jnp.float32
    )


class Exchange:
    def __init__(self, dp, me, far, near, bufs, sems):
        self.dp, self.far, self.near = dp, far, near
        self.z, self.a = lax.div(me, near), lax.rem(me, near)
        self.out0, self.mid0, self.in0, self.out1, self.mid1, self.in1 = bufs
        self.sems = sems

    def copy(self, src, dst, which, z, a):
        return pltpu.make_async_remote_copy(
            src_ref=src,
            dst_ref=dst,
            send_sem=self.sems.at[2 * which],
            recv_sem=self.sems.at[2 * which + 1],
            device_id=(self.dp, z * self.near + a),
            device_id_type=MESH,
        )

    def whole(self, which):
        buf = (self.mid0, self.mid1, self.in0, self.in1)[which]
        others = buf.at[pl.ds(0, buf.shape[0] - 1)]
        return self.copy(others, others, which, self.z, lax.rem(self.a + 1, self.near))

    def own(self, src, dst, which):
        return pltpu.make_async_copy(src, dst, self.sems.at[8 + which])

    def first_hop(self, piece):
        def fill0(z, carry):
            for a in range(self.near):
                self.out0[a, z] = piece(0, z, a)
            return carry

        lax.fori_loop(0, self.far, fill0, 0)

        def send0(k, carry):
            a = lax.rem(self.a + k, self.near)
            self.copy(self.out0.at[a], self.mid0.at[self.a], 0, self.z, a).start()
            return carry

        lax.fori_loop(1, self.near, send0, 0)
        self.own(self.out0.at[self.a], self.mid0.at[self.a], 0).start()

        def fill1(z):
            for a in range(self.near):
                self.out1[z, a] = piece(1, z, a)

        def send1(k, carry):
            z = lax.rem(self.z + k, self.far)
            fill1(z)
            self.copy(self.out1.at[z], self.mid1.at[self.z], 1, z, self.a).start()
            return carry

        lax.fori_loop(1, self.far, send1, 0)
        fill1(self.z)
        self.own(self.out1.at[self.z], self.mid1.at[self.z], 1).start()

    def second_hop(self):
        self.own(self.out0.at[self.a], self.mid0.at[self.a], 0).wait()
        self.whole(0).wait_recv()

        def send0(k, carry):
            z = lax.rem(self.z + k, self.far)
            self.copy(self.mid0.at[:, z], self.in0.at[self.z], 2, z, self.a).start()
            return carry

        lax.fori_loop(1, self.far, send0, 0)
        self.own(self.mid0.at[:, self.z], self.in0.at[self.z], 2).start()

        self.own(self.out1.at[self.z], self.mid1.at[self.z], 1).wait()
        self.whole(1).wait_recv()

        def send1(k, carry):
            a = lax.rem(self.a + k, self.near)
            self.copy(self.mid1.at[:, a], self.in1.at[self.a], 3, self.z, a).start()
            return carry

        lax.fori_loop(1, self.near, send1, 0)
        self.own(self.mid1.at[:, self.a], self.in1.at[self.a], 3).start()

    def wait_slot(self, slot):
        if slot == 0:
            self.own(self.mid0.at[:, self.z], self.in0.at[self.z], 2).wait()
        else:
            self.own(self.mid1.at[:, self.a], self.in1.at[self.a], 3).wait()
        self.whole(2 + slot).wait_recv()

    def arrived(self, slot, z, a):
        return self.in0[z, a] if slot == 0 else self.in1[a, z]

    def finish(self):
        for which in range(4):
            self.whole(which).wait_send()


def soap_kernel(
    dp_count,
    far,
    near,
    owner_slot,
    grad_parts,
    moment,
    second,
    gram_left,
    gram_right,
    basis_left,
    basis_right,
    new_moment,
    new_second,
    new_left,
    new_right,
    update,
    owner_s,
    block_v,
    block_s,
    moment_v,
    second_v,
    left_v,
    right_v,
    basis_left_v,
    basis_right_v,
    partials,
    summed,
    slot_grad,
    slot_update,
    picked,
    load_sems,
    keep_sem,
    partial_send,
    partial_recv,
    gather_send,
    gather_recv,
    out_sems,
    back_sems,
    *buffers,
):
    dp = lax.axis_index("dp")
    me = lax.axis_index("fsdp")
    capacity, side = moment.shape[0], moment.shape[1]
    group_blocks = owner_slot.shape[1]
    rows = grad_parts.shape[2]
    my_z, my_a = lax.div(me, near), lax.rem(me, near)
    outward = Exchange(dp, me, far, near, buffers[:6], out_sems)
    backward = Exchange(dp, me, far, near, buffers[6:], back_sems)

    barrier = pltpu.get_barrier_semaphore()

    def greet(d, f):
        pl.semaphore_signal(barrier, inc=1, device_id=(d, f), device_id_type=MESH)

    for k in range(1, dp_count):
        greet(lax.rem(dp + k, dp_count), me)
    for k in range(1, near):
        greet(dp, my_z * near + lax.rem(my_a + k, near))
    for k in range(1, far):
        greet(dp, lax.rem(my_z + k, far) * near + my_a)

    own_partial = pltpu.make_async_copy(
        grad_parts.at[0, pl.ds(dp * group_blocks, group_blocks)], partials.at[0], load_sems.at[6]
    )
    own_partial.start()
    own_owners = pltpu.make_async_copy(owner_slot, owner_s, load_sems.at[7])
    own_owners.start()
    loads = [
        pltpu.make_async_copy(src, dst, load_sems.at[i])
        for i, (src, dst) in enumerate(
            (
                (basis_left, basis_left_v),
                (basis_right, basis_right_v),
                (moment, moment_v),
                (second, second_v),
                (gram_left, left_v),
                (gram_right, right_v),
            )
        )
    ]
    for load in loads:
        load.start()
    pl.semaphore_wait(barrier, dp_count - 1 + near - 1 + far - 1)

    partial_copies = []
    for k in range(1, dp_count):
        target = lax.rem(dp + k, dp_count)
        copy = pltpu.make_async_remote_copy(
            src_ref=grad_parts.at[0, pl.ds(target * group_blocks, group_blocks)],
            dst_ref=partials.at[k],
            send_sem=partial_send.at[k - 1],
            recv_sem=partial_recv.at[k - 1],
            device_id=(target, me),
            device_id_type=MESH,
        )
        copy.start()
        partial_copies.append(copy)

    own_owners.wait()
    summed[group_blocks] = jnp.zeros(summed.shape[1:], summed.dtype)
    row_slots = near * capacity
    lane = lax.broadcasted_iota(jnp.int32, block_v.shape, 1)
    slot_id = row_slots * lax.broadcasted_iota(jnp.int32, block_v.shape, 0) + lane
    slot_id = jnp.where(lane < row_slots, slot_id, -1)

    def note(i, table):
        for u in range(UNROLL):
            j = i * UNROLL + u
            table = jnp.where(slot_id == owner_s[dp, j], j, table)
        return table

    block_v[...] = lax.fori_loop(
        0, group_blocks // UNROLL, note, jnp.full(block_v.shape, group_blocks, jnp.int32)
    )
    table_copy = pltpu.make_async_copy(block_v, block_s, load_sems.at[8])
    table_copy.start()

    own_partial.wait()
    for copy in partial_copies:
        copy.wait_recv()

    def add_up(i, carry):
        here = pl.ds(i * UNROLL, UNROLL)
        total = partials[0, here].astype(jnp.float32)
        for k in range(1, dp_count):
            total = total + partials[k, here].astype(jnp.float32)
        summed[here] = total.astype(jnp.bfloat16)
        return carry

    lax.fori_loop(0, group_blocks // UNROLL, add_up, 0)
    table_copy.wait()

    def grad_piece(c, z, a):
        return summed[block_s[z, a * capacity + c]]

    outward.first_hop(grad_piece)
    outward.second_hop()

    per_tile = TILE // rows
    tiles_near = near // per_tile

    def unpack(c):
        def far_rows(z, carry):
            for a in range(near):
                u = a % per_tile
                slot_grad[c, z * tiles_near + a // per_tile, u * rows : (u + 1) * rows, :] = (
                    outward.arrived(c, z, a).astype(jnp.float32)
                )
            return carry

        lax.fori_loop(0, far, far_rows, 0)

    for load in loads:
        load.wait()

    rounded = []
    for c in range(capacity):
        outward.wait_slot(c)
        unpack(c)
        rounded.append(slot_grad[c].reshape(side, side).astype(jnp.bfloat16))
        halfway = contract(basis_left_v[c], rounded[c], 0, 0).astype(jnp.bfloat16)
        rotated = contract(halfway, basis_right_v[c], 1, 0)
        first_moment = 0.95 * moment_v[c].astype(jnp.float32) + 0.05 * rotated
        new_moment[c] = first_moment.astype(jnp.bfloat16)
        second_moment = 0.95 * second_v[c] + 0.05 * rotated * rotated
        new_second[c] = second_moment
        direct = (first_moment / (jnp.sqrt(second_moment) + 1e-8)).astype(jnp.bfloat16)
        back = contract(basis_left_v[c], direct, 1, 0).astype(jnp.bfloat16)
        slot_update[c] = contract(back, basis_right_v[c], 1, 1).reshape(slot_update.shape[1:])

    def update_piece(c, z, a):
        u = a % per_tile
        return slot_update[
            c, z * tiles_near + a // per_tile, u * rows : (u + 1) * rows, :
        ].astype(jnp.bfloat16)

    backward.first_hop(update_piece)

    for c in range(capacity):
        new_left[c] = 0.95 * left_v[c] + 0.05 * contract(rounded[c], rounded[c], 1, 1)
        new_right[c] = 0.95 * right_v[c] + 0.05 * contract(rounded[c], rounded[c], 0, 0)
    backward.second_hop()
    for c in range(capacity):
        backward.wait_slot(c)

    def pick(i, carry):
        for u in range(UNROLL):
            j = i * UNROLL + u
            slot = owner_s[dp, j]
            owner = lax.div(slot, capacity)
            z, a = lax.div(owner, near), lax.rem(owner, near)
            first, other = backward.arrived(0, z, a), backward.arrived(1, z, a)
            picked[j] = jnp.where(lax.rem(slot, capacity) == 0, first, other)
        return carry

    lax.fori_loop(0, group_blocks // UNROLL, pick, 0)

    mine = pl.ds(dp * group_blocks, group_blocks)
    gathers = []
    for k in range(1, dp_count):
        copy = pltpu.make_async_remote_copy(
            src_ref=picked,
            dst_ref=update.at[mine],
            send_sem=gather_send.at[k - 1],
            recv_sem=gather_recv.at[k - 1],
            device_id=(lax.rem(dp + k, dp_count), me),
            device_id_type=MESH,
        )
        copy.start()
        gathers.append(copy)
    keep = pltpu.make_async_copy(picked, update.at[mine], keep_sem)
    keep.start()
    outward.finish()
    backward.finish()
    for copy in partial_copies:
        copy.wait_send()
    keep.wait()
    for copy in gathers:
        copy.wait()


def hand_out_kernel(*refs):
    count = len(refs) // 2
    sems = refs[-1]
    copies = [
        pltpu.make_async_copy(src, dst, sems.at[i])
        for i, (src, dst) in enumerate(zip(refs[:count], refs[count : 2 * count]))
    ]
    for copy in copies:
        copy.start()
    for copy in copies:
        copy.wait()


def on_device(
    dp_count,
    fsdp_count,
    grad_parts,
    owner_slot,
    moment,
    second,
    gram_left,
    gram_right,
    basis_left,
    basis_right,
):
    capacity, side = moment.shape[0], moment.shape[1]
    blocks, rows = grad_parts.shape[1], grad_parts.shape[2]
    group_blocks = owner_slot.shape[1]
    far = math.isqrt(fsdp_count // 2)
    near = fsdp_count // far
    any_spec = pl.BlockSpec(memory_space=pl.ANY)
    square = (capacity, side, side)
    tiled = (capacity, side // TILE, TILE, side)
    near_far = pltpu.VMEM((near, far, rows, side), jnp.bfloat16)
    far_near = pltpu.VMEM((far, near, rows, side), jnp.bfloat16)
    table = (-(-far // TILE) * TILE, LANES)
    dma = pltpu.SemaphoreType.DMA
    out_shape = (
        jax.ShapeDtypeStruct(square, jnp.bfloat16),
        jax.ShapeDtypeStruct(square, jnp.float32),
        jax.ShapeDtypeStruct(square, jnp.float32),
        jax.ShapeDtypeStruct(square, jnp.float32),
        jax.ShapeDtypeStruct((blocks, rows, side), jnp.bfloat16),
    )
    results = pl.pallas_call(
        functools.partial(soap_kernel, dp_count, far, near),
        out_shape=tuple(pltpu.VMEM(out.shape, out.dtype) for out in out_shape),
        in_specs=[any_spec] * 8,
        out_specs=[pl.BlockSpec(memory_space=pltpu.VMEM)] * 5,
        scratch_shapes=[
            pltpu.SMEM(owner_slot.shape, jnp.int32),
            pltpu.VMEM(table, jnp.int32),
            pltpu.SMEM(table, jnp.int32),
            pltpu.VMEM(square, jnp.bfloat16),
            pltpu.VMEM(square, jnp.float32),
            pltpu.VMEM(square, jnp.float32),
            pltpu.VMEM(square, jnp.float32),
            pltpu.VMEM(square, jnp.bfloat16),
            pltpu.VMEM(square, jnp.bfloat16),
            pltpu.VMEM((dp_count, group_blocks, rows, side), jnp.bfloat16),
            pltpu.VMEM((group_blocks + 1, rows, side), jnp.bfloat16),
            pltpu.VMEM(tiled, jnp.float32),
            pltpu.VMEM(tiled, jnp.float32),
            pltpu.VMEM((group_blocks, rows, side), jnp.bfloat16),
            dma((9,)),
            dma,
            dma((dp_count - 1,)),
            dma((dp_count - 1,)),
            dma((dp_count - 1,)),
            dma((dp_count - 1,)),
            dma((12,)),
            dma((12,)),
        ]
        + [near_far, near_far, far_near, far_near, far_near, near_far] * 2,
        compiler_params=pltpu.CompilerParams(
            collective_id=0, has_side_effects=True, vmem_limit_bytes=LIMIT * 1024 * 1024
        ),
    )(
        owner_slot,
        grad_parts,
        moment,
        second,
        gram_left,
        gram_right,
        basis_left,
        basis_right,
    )
    return pl.pallas_call(
        hand_out_kernel,
        out_shape=out_shape,
        in_specs=[any_spec] * 5,
        out_specs=[any_spec] * 5,
        scratch_shapes=[dma((5,))],
        compiler_params=pltpu.CompilerParams(vmem_limit_bytes=8 * 1024 * 1024),
    )(*results)


def solution(mesh):
    by_slot = P(("dp", "fsdp"), None, None)
    return jax.shard_map(
        functools.partial(on_device, mesh.shape["dp"], mesh.shape["fsdp"]),
        mesh=mesh,
        in_specs=(P("dp", None, "fsdp", None), P()) + (by_slot,) * 6,
        out_specs=(by_slot,) * 4 + (P(None, "fsdp", None),),
        check_vma=False,
    )
```

time: 67.8 us -> 57.5 us (0.85)
  local copies, waits for them, and re-layouts: 10.8 us -> 0 us
  Pallas kernels: 55.1 us -> 56.7 us
  other arithmetic: 0.88 us -> 0 us
    unnamed x21 -> x0, local copies, waits for them, and re-layouts: 10.8 us -> none
    pallas_call x1 -> x2, Pallas kernels: 55.1 us -> 56.7 us  [the longest x1 55.4 us: on_device(): pl.pallas_call(functools.partial(soap_kernel, dp_count, far, near), out_s...]
    reduce_min x1 -> x0, other arithmetic: 0.88 us -> none  [on_device(): jnp.min(jnp.where(filled, jnp.arange(group_blocks, dtype=jnp.int32)[None,...]
where the time goes in v2:
time: 57.5 us; the launch traced here: 57.4 us
  Pallas kernels  56.7 us (99%)
  between operations  0.64 us (1%)
    pallas_call x1, Pallas kernels, on_device(): pl.pallas_call(functools.partial(soap_kernel, dp_count, far, near), out_s...  55.4 us
    pallas_call x1, Pallas kernels, on_device(): pl.pallas_call(hand_out_kernel, out_shape=out_shape, in_specs=[any_spec]...  1.4 us

profile of v2, /device:TPU:1, one launch (start us, length us, event | category | flops | bytes accessed | tf_op | source)
XLA Modules:
  0.0 57.4 jit_solution(2070358382872342429)
XLA Ops:
  0.6 55.4 %shard_map.119 = (bf16[2,256,256]{2,1,0:T(8,128)(2,1)S(1)}, f32[2,256,256]{2,1,0:T(8,128)S(1)}, f32[2,256,256]{2,1,0:T(8,128)S(1)}, f32[2,256,256]{2,1,0:T(8,128)S(1)}, bf16[384,2,256]{2,1,0:T(2,128)(2,1)S(1)}) custom-call(s32[4,96]{1,0:T(4,128)} %owner_slot.1, bf16[1,384,2,256]{3,2,1,0:T(2,128)(2,1)} %grad_parts.1, bf16[2,256,256]{2,1,0:T(8,128)(2,1)} %moment.1, ...), custom_call_target="tpu_custom_call" | custom-call | tf_op jit(solution)/shard_map/pallas_call | solution.py:383
  56.0 1.4 %shard_map.120 = (bf16[2,256,256]{2,1,0:T(8,128)(2,1)}, f32[2,256,256]{2,1,0:T(8,128)}, f32[2,256,256]{2,1,0:T(8,128)}, f32[2,256,256]{2,1,0:T(8,128)}, bf16[384,2,256]{2,1,0:T(2,128)(2,1)}) custom-call(bf16[2,256,256]{2,1,0:T(8,128)(2,1)S(1)} %get-tuple-element.10.refs_0_, f32[2,256,256]{2,1,0:T(8,128)S(1)} %get-tuple-element.11.refs_1_, ...), custom_call_target="tpu_custom_call" | custom-call | tf_op jit(solution)/shard_map/pallas_call | solution.py:426

commit v3 on v2

--- a/solution.py
+++ b/solution.py
@@ -21,97 +21,61 @@
     )
 
 
+def farthest_first(count, i):
+    out = lax.div(i + 1, 2)
+    return lax.rem(count // 2 + out * (1 - 2 * lax.rem(i, 2)) + count, count)
+
+
 class Exchange:
-    def __init__(self, dp, me, far, near, bufs, sems):
-        self.dp, self.far, self.near = dp, far, near
-        self.z, self.a = lax.div(me, near), lax.rem(me, near)
-        self.out0, self.mid0, self.in0, self.out1, self.mid1, self.in1 = bufs
-        self.sems = sems
-
-    def copy(self, src, dst, which, z, a):
+    def __init__(self, dp, me, far, near, outgoing, incoming, sems):
+        self.dp, self.me, self.far, self.near = dp, me, far, near
+        self.outgoing, self.incoming, self.sems = outgoing, incoming, sems
+        self.span = outgoing.shape[0] // (far * near)
+
+    def copy(self, src, dst, target):
         return pltpu.make_async_remote_copy(
             src_ref=src,
             dst_ref=dst,
-            send_sem=self.sems.at[2 * which],
-            recv_sem=self.sems.at[2 * which + 1],
-            device_id=(self.dp, z * self.near + a),
+            send_sem=self.sems.at[0],
+            recv_sem=self.sems.at[1],
+            device_id=(self.dp, target),
             device_id_type=MESH,
         )
 
-    def whole(self, which):
-        buf = (self.mid0, self.mid1, self.in0, self.in1)[which]
-        others = buf.at[pl.ds(0, buf.shape[0] - 1)]
-        return self.copy(others, others, which, self.z, lax.rem(self.a + 1, self.near))
-
-    def own(self, src, dst, which):
-        return pltpu.make_async_copy(src, dst, self.sems.at[8 + which])
-
-    def first_hop(self, piece):
-        def fill0(z, carry):
-            for a in range(self.near):
-                self.out0[a, z] = piece(0, z, a)
-            return carry
-
-        lax.fori_loop(0, self.far, fill0, 0)
-
-        def send0(k, carry):
-            a = lax.rem(self.a + k, self.near)
-            self.copy(self.out0.at[a], self.mid0.at[self.a], 0, self.z, a).start()
-            return carry
-
-        lax.fori_loop(1, self.near, send0, 0)
-        self.own(self.out0.at[self.a], self.mid0.at[self.a], 0).start()
-
-        def fill1(z):
-            for a in range(self.near):
-                self.out1[z, a] = piece(1, z, a)
-
-        def send1(k, carry):
-            z = lax.rem(self.z + k, self.far)
-            fill1(z)
-            self.copy(self.out1.at[z], self.mid1.at[self.z], 1, z, self.a).start()
-            return carry
-
-        lax.fori_loop(1, self.far, send1, 0)
-        fill1(self.z)
-        self.own(self.out1.at[self.z], self.mid1.at[self.z], 1).start()
-
-    def second_hop(self):
-        self.own(self.out0.at[self.a], self.mid0.at[self.a], 0).wait()
-        self.whole(0).wait_recv()
-
-        def send0(k, carry):
-            z = lax.rem(self.z + k, self.far)
-            self.copy(self.mid0.at[:, z], self.in0.at[self.z], 2, z, self.a).start()
-            return carry
-
-        lax.fori_loop(1, self.far, send0, 0)
-        self.own(self.mid0.at[:, self.z], self.in0.at[self.z], 2).start()
-
-        self.own(self.out1.at[self.z], self.mid1.at[self.z], 1).wait()
-        self.whole(1).wait_recv()
-
-        def send1(k, carry):
-            a = lax.rem(self.a + k, self.near)
-            self.copy(self.mid1.at[:, a], self.in1.at[self.a], 3, self.z, a).start()
-            return carry
-
-        lax.fori_loop(1, self.near, send1, 0)
-        self.own(self.mid1.at[:, self.a], self.in1.at[self.a], 3).start()
-
-    def wait_slot(self, slot):
-        if slot == 0:
-            self.own(self.mid0.at[:, self.z], self.in0.at[self.z], 2).wait()
-        else:
-            self.own(self.mid1.at[:, self.a], self.in1.at[self.a], 3).wait()
-        self.whole(2 + slot).wait_recv()
-
-    def arrived(self, slot, z, a):
-        return self.in0[z, a] if slot == 0 else self.in1[a, z]
-
-    def finish(self):
-        for which in range(4):
-            self.whole(which).wait_send()
+    def send(self, z, a):
+        target = z * self.near + a
+        self.copy(
+            self.outgoing.at[pl.ds(target * self.span, self.span)],
+            self.incoming.at[pl.ds(self.me * self.span, self.span)],
+            target,
+        ).start()
+
+    def start(self, fill):
+        chips = self.near // 2
+        my_z, my_a = lax.div(self.me, self.near), lax.rem(self.me, self.near)
+        my_y, my_core = lax.div(my_a, 2), lax.rem(my_a, 2)
+        for total in range(self.far + chips - 1):
+
+            def step(i, carry):
+                z = lax.rem(my_z + farthest_first(self.far, i), self.far)
+                y = lax.rem(my_y + farthest_first(chips, total - i), chips)
+                for core in (1 - my_core, my_core):
+                    fill(z, 2 * y + core)
+                    self.send(z, 2 * y + core)
+                return carry
+
+            low, high = max(0, total - chips + 1), min(self.far - 1, total)
+            if total < self.far + chips - 2:
+                lax.fori_loop(low, high + 1, step, 0)
+        fill(my_z, 2 * my_y + 1 - my_core)
+        self.send(my_z, 2 * my_y + 1 - my_core)
+        fill(my_z, my_a)
+        for c in range(self.span):
+            self.incoming[self.me * self.span + c] = self.outgoing[self.me * self.span + c]
+
+    def whole(self):
+        others = self.incoming.at[pl.ds(0, (self.far * self.near - 1) * self.span)]
+        return self.copy(others, others, lax.rem(self.me + 1, self.far * self.near))
 
 
 def soap_kernel(
@@ -151,9 +115,13 @@
     partial_recv,
     gather_send,
     gather_recv,
+    ready,
     out_sems,
     back_sems,
-    *buffers,
+    outgoing,
+    incoming,
+    returning,
+    returned,
 ):
     dp = lax.axis_index("dp")
     me = lax.axis_index("fsdp")
@@ -161,8 +129,8 @@
     group_blocks = owner_slot.shape[1]
     rows = grad_parts.shape[2]
     my_z, my_a = lax.div(me, near), lax.rem(me, near)
-    outward = Exchange(dp, me, far, near, buffers[:6], out_sems)
-    backward = Exchange(dp, me, far, near, buffers[6:], back_sems)
+    outward = Exchange(dp, me, far, near, outgoing, incoming, out_sems)
+    backward = Exchange(dp, me, far, near, returning, returned, back_sems)
 
     barrier = pltpu.get_barrier_semaphore()
 
@@ -199,8 +167,9 @@
         load.start()
     pl.semaphore_wait(barrier, dp_count - 1 + near - 1 + far - 1)
 
+    dp_offsets = sorted(range(1, dp_count), key=lambda k: -min(k, dp_count - k))
     partial_copies = []
-    for k in range(1, dp_count):
+    for k in dp_offsets:
         target = lax.rem(dp + k, dp_count)
         copy = pltpu.make_async_remote_copy(
             src_ref=grad_parts.at[0, pl.ds(target * group_blocks, group_blocks)],
@@ -213,6 +182,14 @@
         copy.start()
         partial_copies.append(copy)
 
+    for k in range(1, near):
+        pl.semaphore_signal(
+            ready,
+            inc=1,
+            device_id=(dp, my_z * near + lax.rem(my_a + k, near)),
+            device_id_type=MESH,
+        )
+
     own_owners.wait()
     summed[group_blocks] = jnp.zeros(summed.shape[1:], summed.dtype)
     row_slots = near * capacity
@@ -247,33 +224,33 @@
     lax.fori_loop(0, group_blocks // UNROLL, add_up, 0)
     table_copy.wait()
 
-    def grad_piece(c, z, a):
-        return summed[block_s[z, a * capacity + c]]
-
-    outward.first_hop(grad_piece)
-    outward.second_hop()
+    pl.semaphore_wait(ready, near - 1)
+
+    def fill_grad(z, a):
+        for c in range(capacity):
+            outgoing[(z * near + a) * capacity + c] = summed[block_s[z, a * capacity + c]]
+
+    outward.start(fill_grad)
 
     per_tile = TILE // rows
     tiles_near = near // per_tile
 
-    def unpack(c):
-        def far_rows(z, carry):
-            for a in range(near):
-                u = a % per_tile
-                slot_grad[c, z * tiles_near + a // per_tile, u * rows : (u + 1) * rows, :] = (
-                    outward.arrived(c, z, a).astype(jnp.float32)
-                )
-            return carry
-
-        lax.fori_loop(0, far, far_rows, 0)
+    def unpack(z, carry):
+        for a in range(near):
+            u = a % per_tile
+            for c in range(capacity):
+                slot_grad[c, z * tiles_near + a // per_tile, u * rows : (u + 1) * rows, :] = incoming[
+                    (z * near + a) * capacity + c
+                ].astype(jnp.float32)
+        return carry
 
     for load in loads:
         load.wait()
+    outward.whole().wait_recv()
+    lax.fori_loop(0, far, unpack, 0)
 
     rounded = []
     for c in range(capacity):
-        outward.wait_slot(c)
-        unpack(c)
         rounded.append(slot_grad[c].reshape(side, side).astype(jnp.bfloat16))
         halfway = contract(basis_left_v[c], rounded[c], 0, 0).astype(jnp.bfloat16)
         rotated = contract(halfway, basis_right_v[c], 1, 0)
@@ -285,36 +262,33 @@
         back = contract(basis_left_v[c], direct, 1, 0).astype(jnp.bfloat16)
         slot_update[c] = contract(back, basis_right_v[c], 1, 1).reshape(slot_update.shape[1:])
 
-    def update_piece(c, z, a):
-        u = a % per_tile
-        return slot_update[
-            c, z * tiles_near + a // per_tile, u * rows : (u + 1) * rows, :
-        ].astype(jnp.bfloat16)
-
-    backward.first_hop(update_piece)
+    def pack(z, carry):
+        for a in range(near):
+            u = a % per_tile
+            for c in range(capacity):
+                returning[(z * near + a) * capacity + c] = slot_update[
+                    c, z * tiles_near + a // per_tile, u * rows : (u + 1) * rows, :
+                ].astype(jnp.bfloat16)
+        return carry
+
+    lax.fori_loop(0, far, pack, 0)
+    backward.start(lambda z, a: None)
 
     for c in range(capacity):
         new_left[c] = 0.95 * left_v[c] + 0.05 * contract(rounded[c], rounded[c], 1, 1)
         new_right[c] = 0.95 * right_v[c] + 0.05 * contract(rounded[c], rounded[c], 0, 0)
-    backward.second_hop()
-    for c in range(capacity):
-        backward.wait_slot(c)
+    backward.whole().wait_recv()
 
     def pick(i, carry):
         for u in range(UNROLL):
-            j = i * UNROLL + u
-            slot = owner_s[dp, j]
-            owner = lax.div(slot, capacity)
-            z, a = lax.div(owner, near), lax.rem(owner, near)
-            first, other = backward.arrived(0, z, a), backward.arrived(1, z, a)
-            picked[j] = jnp.where(lax.rem(slot, capacity) == 0, first, other)
+            picked[i * UNROLL + u] = returned[owner_s[dp, i * UNROLL + u]]
         return carry
 
     lax.fori_loop(0, group_blocks // UNROLL, pick, 0)
 
     mine = pl.ds(dp * group_blocks, group_blocks)
     gathers = []
-    for k in range(1, dp_count):
+    for k in dp_offsets:
         copy = pltpu.make_async_remote_copy(
             src_ref=picked,
             dst_ref=update.at[mine],
@@ -327,8 +301,8 @@
         gathers.append(copy)
     keep = pltpu.make_async_copy(picked, update.at[mine], keep_sem)
     keep.start()
-    outward.finish()
-    backward.finish()
+    outward.whole().wait_send()
+    backward.whole().wait_send()
     for copy in partial_copies:
         copy.wait_send()
     keep.wait()
@@ -369,8 +343,7 @@
     any_spec = pl.BlockSpec(memory_space=pl.ANY)
     square = (capacity, side, side)
     tiled = (capacity, side // TILE, TILE, side)
-    near_far = pltpu.VMEM((near, far, rows, side), jnp.bfloat16)
-    far_near = pltpu.VMEM((far, near, rows, side), jnp.bfloat16)
+    by_slot = pltpu.VMEM((fsdp_count * capacity, rows, side), jnp.bfloat16)
     table = (-(-far // TILE) * TILE, LANES)
     dma = pltpu.SemaphoreType.DMA
     out_shape = (
@@ -406,10 +379,14 @@
             dma((dp_count - 1,)),
             dma((dp_count - 1,)),
             dma((dp_count - 1,)),
-            dma((12,)),
-            dma((12,)),
-        ]
-        + [near_far, near_far, far_near, far_near, far_near, near_far] * 2,
+            pltpu.SemaphoreType.REGULAR,
+            dma((2,)),
+            dma((2,)),
+            by_slot,
+            by_slot,
+            by_slot,
+            by_slot,
+        ],
         compiler_params=pltpu.CompilerParams(
             collective_id=0, has_side_effects=True, vmem_limit_bytes=LIMIT * 1024 * 1024
         ),

time: 57.5 us -> 50.6 us (0.88)
  Pallas kernels: 56.7 us -> 49.8 us
    pallas_call x1, Pallas kernels: 55.4 us -> 48.4 us  [on_device(): pl.pallas_call(functools.partial(soap_kernel, dp_count, far, near), out_s...]
where the time goes in v3:
time: 50.6 us; the launch traced here: 50.5 us
  Pallas kernels  49.8 us (98%)
  between operations  0.64 us (1%)
    pallas_call x1, Pallas kernels, on_device(): pl.pallas_call(functools.partial(soap_kernel, dp_count, far, near), out_s...  48.4 us
    pallas_call x1, Pallas kernels, on_device(): pl.pallas_call(hand_out_kernel, out_shape=out_shape, in_specs=[any_spec]...  1.4 us

profile of v3, /device:TPU:1, one launch (start us, length us, event | category | flops | bytes accessed | tf_op | source)
XLA Modules:
  0.0 50.5 jit_solution(704517773174652452)
XLA Ops:
  0.6 48.4 %shard_map.119 = (bf16[2,256,256]{2,1,0:T(8,128)(2,1)S(1)}, f32[2,256,256]{2,1,0:T(8,128)S(1)}, f32[2,256,256]{2,1,0:T(8,128)S(1)}, f32[2,256,256]{2,1,0:T(8,128)S(1)}, bf16[384,2,256]{2,1,0:T(2,128)(2,1)S(1)}) custom-call(s32[4,96]{1,0:T(4,128)} %owner_slot.1, bf16[1,384,2,256]{3,2,1,0:T(2,128)(2,1)} %grad_parts.1, bf16[2,256,256]{2,1,0:T(8,128)(2,1)} %moment.1, ...), custom_call_target="tpu_custom_call" | custom-call | tf_op jit(solution)/shard_map/pallas_call | solution.py:356
  49.1 1.4 %shard_map.120 = (bf16[2,256,256]{2,1,0:T(8,128)(2,1)}, f32[2,256,256]{2,1,0:T(8,128)}, f32[2,256,256]{2,1,0:T(8,128)}, f32[2,256,256]{2,1,0:T(8,128)}, bf16[384,2,256]{2,1,0:T(2,128)(2,1)}) custom-call(bf16[2,256,256]{2,1,0:T(8,128)(2,1)S(1)} %get-tuple-element.10.refs_0_, f32[2,256,256]{2,1,0:T(8,128)S(1)} %get-tuple-element.11.refs_1_, ...), custom_call_target="tpu_custom_call" | custom-call | tf_op jit(solution)/shard_map/pallas_call | solution.py:403

commit v4 on v3

--- a/solution.py
+++ b/solution.py
@@ -13,6 +13,7 @@
 TILE = 8
 LANES = 128
 LIMIT = 60
+PLANES = (1, 1, 1, 1, 4)
 
 
 def contract(a, b, a_dim, b_dim):
@@ -70,6 +71,29 @@
         fill(my_z, 2 * my_y + 1 - my_core)
         self.send(my_z, 2 * my_y + 1 - my_core)
         fill(my_z, my_a)
+        for c in range(self.span):
+            self.incoming[self.me * self.span + c] = self.outgoing[self.me * self.span + c]
+
+    def start_by_z(self):
+        chips = self.near // 2
+        my_z, my_a = lax.div(self.me, self.near), lax.rem(self.me, self.near)
+        my_y, my_core = lax.div(my_a, 2), lax.rem(my_a, 2)
+        first = 0
+        for planes in PLANES if sum(PLANES) == self.far else (1,) * self.far:
+
+            def step(i, carry):
+                z = first + lax.rem(my_z + i, planes)
+                y = lax.rem(my_y + farthest_first(chips, lax.div(i, planes)), chips)
+                self.send(z, 2 * y + 1 - my_core)
+
+                @pl.when(jnp.logical_or(z != my_z, y != my_y))
+                def _():
+                    self.send(z, 2 * y + my_core)
+
+                return carry
+
+            lax.fori_loop(0, planes * chips, step, 0)
+            first += planes
         for c in range(self.span):
             self.incoming[self.me * self.span + c] = self.outgoing[self.me * self.span + c]
 
@@ -272,7 +296,7 @@
         return carry
 
     lax.fori_loop(0, far, pack, 0)
-    backward.start(lambda z, a: None)
+    backward.start_by_z()
 
     for c in range(capacity):
         new_left[c] = 0.95 * left_v[c] + 0.05 * contract(rounded[c], rounded[c], 1, 1)

time: 50.6 us -> 48.2 us (0.953)
  Pallas kernels: 49.8 us -> 47 us
    pallas_call x1, Pallas kernels: 48.4 us -> 45.6 us  [on_device(): pl.pallas_call(functools.partial(soap_kernel, dp_count, far, near), out_s...]
where the time goes in v4:
time: 48.2 us; the launch traced here: 47.7 us
  Pallas kernels  47 us (98%)
  between operations  0.64 us (1%)
    pallas_call x1, Pallas kernels, on_device(): pl.pallas_call(functools.partial(soap_kernel, dp_count, far, near), out_s...  45.6 us
    pallas_call x1, Pallas kernels, on_device(): pl.pallas_call(hand_out_kernel, out_shape=out_shape, in_specs=[any_spec]...  1.4 us

profile of v4, /device:TPU:1, one launch (start us, length us, event | category | flops | bytes accessed | tf_op | source)
XLA Modules:
  0.0 47.7 jit_solution(16873967357393563050)
XLA Ops:
  0.6 45.6 %shard_map.119 = (bf16[2,256,256]{2,1,0:T(8,128)(2,1)S(1)}, f32[2,256,256]{2,1,0:T(8,128)S(1)}, f32[2,256,256]{2,1,0:T(8,128)S(1)}, f32[2,256,256]{2,1,0:T(8,128)S(1)}, bf16[384,2,256]{2,1,0:T(2,128)(2,1)S(1)}) custom-call(s32[4,96]{1,0:T(4,128)} %owner_slot.1, bf16[1,384,2,256]{3,2,1,0:T(2,128)(2,1)} %grad_parts.1, bf16[2,256,256]{2,1,0:T(8,128)(2,1)} %moment.1, ...), custom_call_target="tpu_custom_call" | custom-call | tf_op jit(solution)/shard_map/pallas_call | solution.py:380
  46.3 1.4 %shard_map.120 = (bf16[2,256,256]{2,1,0:T(8,128)(2,1)}, f32[2,256,256]{2,1,0:T(8,128)}, f32[2,256,256]{2,1,0:T(8,128)}, f32[2,256,256]{2,1,0:T(8,128)}, bf16[384,2,256]{2,1,0:T(2,128)(2,1)}) custom-call(bf16[2,256,256]{2,1,0:T(8,128)(2,1)S(1)} %get-tuple-element.10.refs_0_, f32[2,256,256]{2,1,0:T(8,128)S(1)} %get-tuple-element.11.refs_1_, ...), custom_call_target="tpu_custom_call" | custom-call | tf_op jit(solution)/shard_map/pallas_call | solution.py:427

commit v5 on v4

--- a/solution.py
+++ b/solution.py
@@ -273,18 +273,20 @@
     outward.whole().wait_recv()
     lax.fori_loop(0, far, unpack, 0)
 
-    rounded = []
-    for c in range(capacity):
-        rounded.append(slot_grad[c].reshape(side, side).astype(jnp.bfloat16))
-        halfway = contract(basis_left_v[c], rounded[c], 0, 0).astype(jnp.bfloat16)
-        rotated = contract(halfway, basis_right_v[c], 1, 0)
-        first_moment = 0.95 * moment_v[c].astype(jnp.float32) + 0.05 * rotated
+    every = range(capacity)
+    rounded = [slot_grad[c].reshape(side, side).astype(jnp.bfloat16) for c in every]
+    halfway = [contract(basis_left_v[c], rounded[c], 0, 0).astype(jnp.bfloat16) for c in every]
+    rotated = [contract(halfway[c], basis_right_v[c], 1, 0) for c in every]
+    direct = []
+    for c in every:
+        first_moment = 0.95 * moment_v[c].astype(jnp.float32) + 0.05 * rotated[c]
+        second_moment = 0.95 * second_v[c] + 0.05 * rotated[c] * rotated[c]
         new_moment[c] = first_moment.astype(jnp.bfloat16)
-        second_moment = 0.95 * second_v[c] + 0.05 * rotated * rotated
         new_second[c] = second_moment
-        direct = (first_moment / (jnp.sqrt(second_moment) + 1e-8)).astype(jnp.bfloat16)
-        back = contract(basis_left_v[c], direct, 1, 0).astype(jnp.bfloat16)
-        slot_update[c] = contract(back, basis_right_v[c], 1, 1).reshape(slot_update.shape[1:])
+        direct.append((first_moment / (jnp.sqrt(second_moment) + 1e-8)).astype(jnp.bfloat16))
+    back = [contract(basis_left_v[c], direct[c], 1, 0).astype(jnp.bfloat16) for c in every]
+    for c in every:
+        slot_update[c] = contract(back[c], basis_right_v[c], 1, 1).reshape(slot_update.shape[1:])
 
     def pack(z, carry):
         for a in range(near):

time: 48.2 us -> 47.9 us (level)
  no operation moved by 1% of the time
where the time goes in v5:
time: 47.9 us; the launch traced here: 47.4 us
  Pallas kernels  46.8 us (98%)
  between operations  0.64 us (1%)
    pallas_call x1, Pallas kernels, on_device(): pl.pallas_call(functools.partial(soap_kernel, dp_count, far, near), out_s...  45.4 us
    pallas_call x1, Pallas kernels, on_device(): pl.pallas_call(hand_out_kernel, out_shape=out_shape, in_specs=[any_spec]...  1.4 us

profile of v5, /device:TPU:1, one launch (start us, length us, event | category | flops | bytes accessed | tf_op | source)
XLA Modules:
  0.0 47.4 jit_solution(1611672231927963061)
XLA Ops:
  0.6 45.4 %shard_map.119 = (bf16[2,256,256]{2,1,0:T(8,128)(2,1)S(1)}, f32[2,256,256]{2,1,0:T(8,128)S(1)}, f32[2,256,256]{2,1,0:T(8,128)S(1)}, f32[2,256,256]{2,1,0:T(8,128)S(1)}, bf16[384,2,256]{2,1,0:T(2,128)(2,1)S(1)}) custom-call(s32[4,96]{1,0:T(4,128)} %owner_slot.1, bf16[1,384,2,256]{3,2,1,0:T(2,128)(2,1)} %grad_parts.1, bf16[2,256,256]{2,1,0:T(8,128)(2,1)} %moment.1, ...), custom_call_target="tpu_custom_call" | custom-call | tf_op jit(solution)/shard_map/pallas_call | solution.py:382
  46.0 1.4 %shard_map.120 = (bf16[2,256,256]{2,1,0:T(8,128)(2,1)}, f32[2,256,256]{2,1,0:T(8,128)}, f32[2,256,256]{2,1,0:T(8,128)}, f32[2,256,256]{2,1,0:T(8,128)}, bf16[384,2,256]{2,1,0:T(2,128)(2,1)}) custom-call(bf16[2,256,256]{2,1,0:T(8,128)(2,1)S(1)} %get-tuple-element.10.refs_0_, f32[2,256,256]{2,1,0:T(8,128)S(1)} %get-tuple-element.11.refs_1_, ...), custom_call_target="tpu_custom_call" | custom-call | tf_op jit(solution)/shard_map/pallas_call | solution.py:429
